TPU v7x, 32 devices: a whole 2x2x4 slice. The times are simulated.
32 devices in a mesh: member: 8 (over z, y), fsdp: 4 (over x, core).
Axes of the slice: x: 2, y: 2, z: 4, core: 2. Of those that a mesh axis runs over, the one named last changes fastest.
Arguments:
- probe_acts: bfloat16 [8, 4, 224, 4096], P('member', 'fsdp'), may hold values from -6 to 6
- member_weight: bfloat16 [8, 4096, 1792], P('member', 'fsdp'), may hold values from -6 to 6
- gate_values: bfloat16 [8, 4, 224, 1792], P('member', 'fsdp'), may hold values from -6 to 6
- out_grad: bfloat16 [8, 4, 224, 1792], P('member', 'fsdp'), may hold values from -6 to 6
- loss_mask: int32 [4, 224], P('fsdp'), may hold values 0 or 1
Outputs:
- merged: bfloat16 [4096, 1792], P(None, 'member')
- fisher_mean: float32 [4096, 1792], P('fsdp', 'member')
All inputs are finite; a program needn't handle non-finite values. No bound on the sum of `loss_mask` on one device may be relied on, other than what follows from the above.
Results may differ from a plain program's by a relative error of at most 0.0045.
Values may be sent and summed in bfloat16 or wider, within the bound.
A program may use at most 128 MiB of HBM per device.

v0:
```python
import jax
import jax.numpy as jnp
from jax import lax
from jax.sharding import PartitionSpec as P


def shards(probe_acts, member_weight, gate_values, out_grad, loss_mask):
    acts_local = probe_acts[0]
    weight_shard = member_weight[0]
    own_rows = weight_shard.shape[0]
    width_cols = weight_shard.shape[1]
    seq_len = acts_local.shape[1]
    gate_act = jax.nn.silu(gate_values[0].astype(jnp.float32))
    mask_float = loss_mask.astype(jnp.float32)[:, :, None]
    cotangent = (mask_float * out_grad[0].astype(jnp.float32) * gate_act).astype(jnp.bfloat16)
    columns = lax.all_to_all(acts_local, "fsdp", split_axis=2, concat_axis=0, tiled=True)
    norm_factor = 1.0 / (columns.shape[0] * seq_len)
    zeros_block = jnp.zeros((own_rows, width_cols), jnp.float32)
    all_cotangents = lax.all_gather(cotangent, "fsdp", axis=0, tiled=True)

    def add_example(index, acc):
        acts_one = lax.dynamic_index_in_dim(columns, 0 + index, 0, keepdims=False)
        cot_one = lax.dynamic_index_in_dim(all_cotangents, index, 0, keepdims=False)
        grads = jnp.einsum("lr,lc->rc", acts_one, cot_one, preferred_element_type=jnp.float32)
        return acc + grads * grads

    squares = lax.fori_loop(0, all_cotangents.shape[0], add_example, zeros_block)
    fisher = squares * norm_factor
    weighted_term = fisher * weight_shard.astype(jnp.float32)
    share_cols = width_cols // lax.axis_size("member")
    total_full, weighted_full = lax.psum((fisher, weighted_term), "member")
    first_col = lax.axis_index("member") * share_cols
    fisher_total = lax.dynamic_slice_in_dim(total_full, first_col, share_cols, 1)
    weighted = lax.dynamic_slice_in_dim(weighted_full, first_col, share_cols, 1)
    merged_part = (weighted / (fisher_total + 1e-06)).astype(jnp.bfloat16)
    merged = lax.all_gather(merged_part, "fsdp", axis=0, tiled=True)
    fisher_mean = fisher_total / lax.axis_size("member")
    return (merged, fisher_mean)


def solution(mesh):
    in_specs = (
        P("member", "fsdp", None, None),
        P("member", "fsdp", None),
        P("member", "fsdp", None, None),
        P("member", "fsdp", None, None),
        P("fsdp", None),
    )
    out_specs = (P(None, "member"), P("fsdp", "member"))
    return jax.shard_map(shards, mesh=mesh, in_specs=in_specs, out_specs=out_specs, check_vma=False)
```

profile of v0, /device:TPU:0, one launch (start us, length us, event | category | flops | bytes accessed | tf_op | source)
XLA Modules:
  0.0 622.8 jit_solution(4245465798634222640)
XLA Ops:
  7.2 0.0 copy-start
  7.2 0.0 all-gather.3.cloned.1.call-start
  7.2 0.8 convert_element_type.53
  8.0 2.8 fusion.9
  10.9 0.0 all-gather.3.cloned.1.call-update
  10.9 0.0 copy-done
  10.9 8.6 %copy.17 = bf16[1,224,4096]{1,0,2:T(2,128)(2,1)} copy(bf16[1,224,4096]{2,1,0:T(8,128)(2,1)S(1)} %bitcast.31) | data formatting | bytes 3670016 | tf_op jit(solution)/shard_map/squeeze | solution.py:8
  19.5 0.5 broadcast.46
  20.0 23.7 %reduce = bf16[4096,224]{1,0:T(8,128)(2,1)S(1)} reduce(bf16[4096,1,224]{2,1,0:T(2,128)(2,1)} %bitcast.27, bf16[]{:T(256)} %broadcast.46), dimensions={1}, to_apply=%bitcast.21.reduce_sub_computation | reduce | bytes 3670018
  43.7 4.3 reshape.97
  48.0 4.2 all-to-all-start
  52.2 0.0 all-reduce.3.cloned.1.call-start
  52.2 5.9 copy.21
  58.2 17.0 %all-to-all-done = bf16[4,2,114688]{2,1,0:T(2,128)(2,1)S(1)} async-done(((bf16[4,2,114688]{2,1,0:T(2,128)(2,1)}), bf16[4,2,114688]{2,1,0:T(2,128)(2,1)S(1)}, u32[]{:S(2)}, u32[]{:S(2)}) %all-to-all-start) | async-done | bytes 1835040 | tf_op jit(solution)/shard_map/all_to_all | solution.py:16
  75.2 5.2 reshape.98
  80.3 2.5 copy.23
  82.9 2.4 copy.22
  85.3 2.0 copy.19
  87.3 0.0 all-gather.3.cloned.1.call-done
  87.4 27.7 %while.14 = (s32[]{:T(128)}, f32[1024,1792]{1,0:T(8,128)}, bf16[4,224,1024]{2,1,0:T(8,128)(2,1)S(1)}, bf16[4,224,1792]{2,1,0:T(8,128)(2,1)}, s32[]{:T(128)}, /*index=5*/s32[]{:T(128)}) while((s32[]{:T(128)}, f32[1024,1792]{1,0:T(8,128)}, bf16[4,224,1024]{2,1,0:T(8,128)(2,1)S(1)}, bf16[4,224,1792]{2,1,0:T(8,128)(2,1)}, s32[]{:T(128)}, ...), condition=%wide.region_1.2_spmd.clone, body=%wide.region_0.1_spmd.clone.sunk | while | flops 827588608 | bytes 15943254 | solution.py:27
  87.4 5.3 select_add_fusion.2
  92.7 7.5 %select_add_fusion.2 = f32[1024,1792]{1,0:T(8,128)} fusion(f32[1024,1792]{1,0:T(8,128)} %get-tuple-element.155, pred[]{:T(512)S(6)} %compare.3, bf16[4,224,1792]{2,1,0:T(8,128)(2,1)} %get-tuple-element.163, s32[]{:T(128)S(6)} %copy.26, bf16[4,224,1024]{2,1,0:T(8,128)(2,1)S(1)} %get-tuple-element.162), kind=kOutput, calls=%fused_computation.clone.1 | convolution fusion | flops 827588608 | bytes 15943168 | tf_op jit(solution)/shard_map/while/body/eval_jaxpr/lr,lc->rc/dot_general | solution.py:24
  100.1 7.5 %select_add_fusion.2 = f32[1024,1792]{1,0:T(8,128)} fusion(f32[1024,1792]{1,0:T(8,128)} %get-tuple-element.155, pred[]{:T(512)S(6)} %compare.3, bf16[4,224,1792]{2,1,0:T(8,128)(2,1)} %get-tuple-element.163, s32[]{:T(128)S(6)} %copy.26, bf16[4,224,1024]{2,1,0:T(8,128)(2,1)S(1)} %get-tuple-element.162), kind=kOutput, calls=%fused_computation.clone.1 | convolution fusion | flops 827588608 | bytes 15943168 | tf_op jit(solution)/shard_map/while/body/eval_jaxpr/lr,lc->rc/dot_general | solution.py:24
  107.6 7.5 %select_add_fusion.2 = f32[1024,1792]{1,0:T(8,128)} fusion(f32[1024,1792]{1,0:T(8,128)} %get-tuple-element.155, pred[]{:T(512)S(6)} %compare.3, bf16[4,224,1792]{2,1,0:T(8,128)(2,1)} %get-tuple-element.163, s32[]{:T(128)S(6)} %copy.26, bf16[4,224,1024]{2,1,0:T(8,128)(2,1)S(1)} %get-tuple-element.162), kind=kOutput, calls=%fused_computation.clone.1 | convolution fusion | flops 827588608 | bytes 15943168 | tf_op jit(solution)/shard_map/while/body/eval_jaxpr/lr,lc->rc/dot_general | solution.py:24
  115.1 8.4 %copy.20 = f32[1024,1792]{0,1:T(8,128)} copy(f32[1024,1792]{1,0:T(8,128)} %get-tuple-element.81) | data formatting | bytes 14680064 | tf_op jit(solution)/shard_map/while | solution.py:27
  123.5 12.1 %broadcast_multiply_fusion = (f32[1024,1792]{0,1:T(8,128)}, f32[1024,1792]{0,1:T(8,128)}) fusion(f32[1024,1792]{0,1:T(8,128)} %copy.20, bf16[1,1024,1792]{1,2,0:T(8,128)(2,1)} %copy.21), kind=kLoop, calls=%fused_computation.7 | loop fusion | flops 5505024 | bytes 25690112 | tf_op jit(solution)/shard_map/mul | solution.py:28
  135.6 0.0 all-reduce.3.cloned.1.call-update
  135.6 0.0 all-gather.5.cloned.1.call-start
  135.7 454.5 %all-reduce.3.cloned.1.call-done = (f32[1024,1792]{0,1:T(8,128)}, f32[1024,1792]{0,1:T(8,128)}) async-done(((f32[1024,1792]{0,1:T(8,128)}, f32[1024,1792]{0,1:T(8,128)}), (f32[1024,1792]{0,1:T(8,128)}, f32[1024,1792]{0,1:T(8,128)})) %all-reduce.3.cloned.1.call-update) | async-done | bytes 14680080 | tf_op jit(solution)/shard_map/psum | solution.py:31
  590.2 2.8 dynamic-slice_multiply_fusion
  593.0 0.0 all-gather.5.cloned.1.call-update
  593.0 20.3 %all-gather.5.cloned.1.call-done = bf16[4096,224]{0,1:T(8,128)(2,1)} async-done(((bf16[1024,224]{0,1:T(8,128)(2,1)}), bf16[4096,224]{0,1:T(8,128)(2,1)}) %all-gather.5.cloned.1.call-update) | async-done | bytes 1835024 | tf_op jit(solution)/shard_map/all_gather | solution.py:36
  613.3 2.9 copy.33
  (1 shorter events, 0.0 us)
Async XLA Ops:
  7.2 3.7 copy-start
  7.2 80.2 %all-gather.3.cloned.1.call-start = ((), (), s32[]{:S(2)}) async-start(), calls=%async_computation.1 | async-start | bytes 4014080 | tf_op jit(solution)/shard_map/all_gather | solution.py:19
  48.0 27.2 %all-to-all-start = ((bf16[4,2,114688]{2,1,0:T(2,128)(2,1)}), bf16[4,2,114688]{2,1,0:T(2,128)(2,1)S(1)}, u32[]{:S(2)}, u32[]{:S(2)}) async-start(bf16[4,2,114688]{2,1,0:T(2,128)(2,1)} %reshape.97), calls=%async_computation | async-start | bytes 3670016 | tf_op jit(solution)/shard_map/all_to_all | solution.py:16
  52.2 538.0 %all-reduce.3.cloned.1.call-start = ((), (), s32[]{:S(2)}) async-start(), calls=%async_computation.3 | async-start | bytes 29360128 | tf_op jit(solution)/shard_map/psum | solution.py:31
  135.6 477.7 %all-gather.5.cloned.1.call-start = ((), (), s32[]{:S(2)}) async-start(), calls=%async_computation.2 | async-start | bytes 2293760 | tf_op jit(solution)/shard_map/all_gather | solution.py:36
Sparse Core Ops, SparseCore 0:
  11.0 31.5 all-gather.2
  135.8 454.4 all-reduce.2
  593.1 20.1 all-gather.4
where the time goes:
time: 623 us
  waiting for transfers between devices  492 us (79%)
  local copies, waits for them, and re-layouts  42.8 us (7%)
  other arithmetic  42.2 us (7%)
  matrix products  27.7 us (4%)
  between operations  13.8 us (2%)
    psum x1, waiting for transfers between devices, shards(): total_full, weighted_full = lax.psum((fisher, weighted_term), 'member')  455 us
    dot_general x4, matrix products, add_example(): jnp.einsum('lr,lc->rc', acts_one, cot_one, preferred_element_type=jnp.flo...  27.7 us
    unnamed x2, other arithmetic  23.7 us
    unnamed x9, local copies, waits for them, and re-layouts  23.5 us
    all_gather x1, waiting for transfers between devices, shards(): merged = lax.all_gather(merged_part, 'fsdp', axis=0, tiled=True)  20.3 us
    all_to_all x1, waiting for transfers between devices, shards(): lax.all_to_all(acts_local, 'fsdp', split_axis=2, concat_axis=0, tiled=True)  17 us
  transfers between devices with their start and end apart: 4, of which 3 were waited for; matrix products, arithmetic and copies ran while one was open for 9% of the time, Pallas kernels for 0%

commit v1 on v0

--- a/solution.py
+++ b/solution.py
@@ -13,7 +13,12 @@
     gate_act = jax.nn.silu(gate_values[0].astype(jnp.float32))
     mask_float = loss_mask.astype(jnp.float32)[:, :, None]
     cotangent = (mask_float * out_grad[0].astype(jnp.float32) * gate_act).astype(jnp.bfloat16)
-    columns = lax.all_to_all(acts_local, "fsdp", split_axis=2, concat_axis=0, tiled=True)
+    columns = jnp.concatenate(
+        lax.all_to_all(
+            jnp.stack(jnp.split(acts_local, lax.axis_size("fsdp"), axis=2)), "fsdp", 0, 0
+        ),
+        axis=0,
+    )
     norm_factor = 1.0 / (columns.shape[0] * seq_len)
     zeros_block = jnp.zeros((own_rows, width_cols), jnp.float32)
     all_cotangents = lax.all_gather(cotangent, "fsdp", axis=0, tiled=True)

time: 623 us -> 594 us (0.953)
  local copies, waits for them, and re-layouts: 42.8 us -> 17.5 us
  other arithmetic: 42.2 us -> 20 us
  waiting for transfers between devices: 492 us -> 511 us
    unnamed x2 -> x1, other arithmetic: 23.7 us -> 0.01 us
    all_to_all x1, waiting for transfers between devices: 17 us -> 33.3 us  [shards(): lax.all_to_all(jnp.stack(jnp.split(acts_local, lax.axis_size('fsdp'), axi...]
    unnamed x9 -> x4, local copies, waits for them, and re-layouts: 23.5 us -> 8.93 us
    squeeze x1 -> x0, local copies, waits for them, and re-layouts: 8.55 us -> none  [shards(): acts_local = probe_acts[0]]
  transfers between devices with their start and end apart: 4 -> 4, of which waited for: 3 -> 4; matrix products, arithmetic and copies ran while one was open for 9% -> 1% of each run, Pallas kernels for 0% -> 0%
where the time goes in v1:
time: 594 us
  waiting for transfers between devices  511 us (86%)
  matrix products  27.7 us (5%)
  other arithmetic  20 us (3%)
  local copies, waits for them, and re-layouts  17.5 us (3%)
  between operations  13.8 us (2%)
    psum x1, waiting for transfers between devices, shards(): total_full, weighted_full = lax.psum((fisher, weighted_term), 'member')  455 us
    all_to_all x1, waiting for transfers between devices, shards(): lax.all_to_all(jnp.stack(jnp.split(acts_local, lax.axis_size('fsdp'), axi...  33.3 us
    dot_general x4, matrix products, add_example(): jnp.einsum('lr,lc->rc', acts_one, cot_one, preferred_element_type=jnp.flo...  27.7 us
    all_gather x1, waiting for transfers between devices, shards(): merged = lax.all_gather(merged_part, 'fsdp', axis=0, tiled=True)  20.3 us
    mul x1, other arithmetic, shards(): fisher = squares * norm_factor  12.1 us
  transfers between devices with their start and end apart: 4, of which 4 were waited for; matrix products, arithmetic and copies ran while one was open for 1% of the time, Pallas kernels for 0%

profile of v1, /device:TPU:0, one launch (start us, length us, event | category | flops | bytes accessed | tf_op | source)
XLA Modules:
  0.0 593.9 jit_solution(10195035385518618891)
XLA Ops:
  7.2 0.0 copy-start
  7.2 0.0 all-gather.3.cloned.1.call-start
  7.2 0.8 convert_element_type.53
  8.0 2.8 fusion.9
  10.9 0.0 all-gather.3.cloned.1.call-update
  10.9 0.0 copy-done
  10.9 0.1 slice_bitcast_fusion.3
  11.1 1.5 pad_maximum_fusion
  12.5 4.2 all-to-all-start
  16.7 0.0 all-reduce.3.cloned.1.call-start
  16.7 6.0 %copy.13 = bf16[1,1024,1792]{1,2,0:T(8,128)(2,1)} copy(bf16[1,1024,1792]{2,1,0:T(8,128)(2,1)} %param.8) | data formatting | bytes 7340032 | tf_op args[1]
  22.7 33.3 %all-to-all-done = bf16[4,1,224,1024]{3,2,1,0:T(8,128)(2,1)S(1)} async-done(((bf16[4,1,224,1024]{3,2,1,0:T(8,128)(2,1)}), bf16[4,1,224,1024]{3,2,1,0:T(8,128)(2,1)S(1)}, u32[]{:S(2)}, u32[]{:S(2)}) %all-to-all-start) | async-done | bytes 1835040 | tf_op jit(solution)/shard_map/all_to_all | solution.py:17
  56.0 2.4 all-gather.3.cloned.1.call-done
  58.4 27.7 %while.14 = (s32[]{:T(128)}, f32[1024,1792]{1,0:T(8,128)}, bf16[4,224,1024]{2,1,0:T(8,128)(2,1)S(1)}, bf16[4,224,1792]{2,1,0:T(8,128)(2,1)}, s32[]{:T(128)}, /*index=5*/s32[]{:T(128)}) while((s32[]{:T(128)}, f32[1024,1792]{1,0:T(8,128)}, bf16[4,224,1024]{2,1,0:T(8,128)(2,1)S(1)}, bf16[4,224,1792]{2,1,0:T(8,128)(2,1)}, s32[]{:T(128)}, ...), condition=%wide.region_1.2_spmd.clone, body=%wide.region_0.1_spmd.clone.sunk | while | flops 827588608 | bytes 15942735 | solution.py:32
  58.4 5.3 select_add_fusion.2
  63.7 7.5 %select_add_fusion.2 = f32[1024,1792]{1,0:T(8,128)} fusion(f32[1024,1792]{1,0:T(8,128)} %get-tuple-element.147, pred[]{:T(512)S(6)} %compare.3, bf16[4,224,1792]{2,1,0:T(8,128)(2,1)} %get-tuple-element.155, s32[]{:T(128)} %get-tuple-element.146, bf16[4,224,1024]{2,1,0:T(8,128)(2,1)S(1)} %get-tuple-element.154), kind=kOutput, calls=%fused_computation.clone.1 | convolution fusion | flops 827588608 | bytes 15942657 | tf_op jit(solution)/shard_map/while/body/eval_jaxpr/lr,lc->rc/dot_general | solution.py:29
  71.1 7.5 %select_add_fusion.2 = f32[1024,1792]{1,0:T(8,128)} fusion(f32[1024,1792]{1,0:T(8,128)} %get-tuple-element.147, pred[]{:T(512)S(6)} %compare.3, bf16[4,224,1792]{2,1,0:T(8,128)(2,1)} %get-tuple-element.155, s32[]{:T(128)} %get-tuple-element.146, bf16[4,224,1024]{2,1,0:T(8,128)(2,1)S(1)} %get-tuple-element.154), kind=kOutput, calls=%fused_computation.clone.1 | convolution fusion | flops 827588608 | bytes 15942657 | tf_op jit(solution)/shard_map/while/body/eval_jaxpr/lr,lc->rc/dot_general | solution.py:29
  78.6 7.5 %select_add_fusion.2 = f32[1024,1792]{1,0:T(8,128)} fusion(f32[1024,1792]{1,0:T(8,128)} %get-tuple-element.147, pred[]{:T(512)S(6)} %compare.3, bf16[4,224,1792]{2,1,0:T(8,128)(2,1)} %get-tuple-element.155, s32[]{:T(128)} %get-tuple-element.146, bf16[4,224,1024]{2,1,0:T(8,128)(2,1)S(1)} %get-tuple-element.154), kind=kOutput, calls=%fused_computation.clone.1 | convolution fusion | flops 827588608 | bytes 15942657 | tf_op jit(solution)/shard_map/while/body/eval_jaxpr/lr,lc->rc/dot_general | solution.py:29
  86.1 8.4 %copy.12 = f32[1024,1792]{0,1:T(8,128)} copy(f32[1024,1792]{1,0:T(8,128)} %get-tuple-element.81) | data formatting | bytes 14680064 | tf_op jit(solution)/shard_map/while | solution.py:32
  94.4 12.1 %broadcast_multiply_fusion = (f32[1024,1792]{0,1:T(8,128)}, f32[1024,1792]{0,1:T(8,128)}) fusion(f32[1024,1792]{0,1:T(8,128)} %copy.12, bf16[1,1024,1792]{1,2,0:T(8,128)(2,1)} %copy.13), kind=kLoop, calls=%fused_computation.7 | loop fusion | flops 5505024 | bytes 25690112 | tf_op jit(solution)/shard_map/mul | solution.py:33
  106.6 0.0 all-reduce.3.cloned.1.call-update
  106.6 0.0 all-gather.5.cloned.1.call-start
  106.7 454.6 %all-reduce.3.cloned.1.call-done = (f32[1024,1792]{0,1:T(8,128)}, f32[1024,1792]{0,1:T(8,128)}) async-done(((f32[1024,1792]{0,1:T(8,128)}, f32[1024,1792]{0,1:T(8,128)}), (f32[1024,1792]{0,1:T(8,128)}, f32[1024,1792]{0,1:T(8,128)})) %all-reduce.3.cloned.1.call-update) | async-done | bytes 14680080 | tf_op jit(solution)/shard_map/psum | solution.py:36
  561.3 2.8 dynamic-slice_multiply_fusion
  564.1 0.0 all-gather.5.cloned.1.call-update
  564.1 20.3 %all-gather.5.cloned.1.call-done = bf16[4096,224]{0,1:T(8,128)(2,1)} async-done(((bf16[1024,224]{0,1:T(8,128)(2,1)}), bf16[4096,224]{0,1:T(8,128)(2,1)}) %all-gather.5.cloned.1.call-update) | async-done | bytes 1835024 | tf_op jit(solution)/shard_map/all_gather | solution.py:41
  584.4 2.9 copy.23
  (1 shorter events, 0.0 us)
Async XLA Ops:
  7.2 3.7 copy-start
  7.2 51.2 %all-gather.3.cloned.1.call-start = ((), (), s32[]{:S(2)}) async-start(), calls=%async_computation.1 | async-start | bytes 4014080 | tf_op jit(solution)/shard_map/all_gather | solution.py:24
  12.5 43.5 %all-to-all-start = ((bf16[4,1,224,1024]{3,2,1,0:T(8,128)(2,1)}), bf16[4,1,224,1024]{3,2,1,0:T(8,128)(2,1)S(1)}, u32[]{:S(2)}, u32[]{:S(2)}) async-start(bf16[4,1,224,1024]{3,2,1,0:T(8,128)(2,1)} %pad_maximum_fusion), calls=%async_computation | async-start | bytes 3670016 | tf_op jit(solution)/shard_map/all_to_all | solution.py:17
  16.7 544.6 %all-reduce.3.cloned.1.call-start = ((), (), s32[]{:S(2)}) async-start(), calls=%async_computation.3 | async-start | bytes 29360128 | tf_op jit(solution)/shard_map/psum | solution.py:36
  106.6 477.8 %all-gather.5.cloned.1.call-start = ((), (), s32[]{:S(2)}) async-start(), calls=%async_computation.2 | async-start | bytes 2293760 | tf_op jit(solution)/shard_map/all_gather | solution.py:41
Sparse Core Ops, SparseCore 0:
  11.0 47.3 all-gather.2
  106.7 454.5 all-reduce.2
  564.2 20.1 all-gather.4
